TPU v7x, 32 devices: a whole 2x2x4 slice. The times are simulated.
32 devices in a mesh: req: 8 (over z, x), head: 4 (over y, core).
Axes of the slice: x: 2, y: 2, z: 4, core: 2. Of those that a mesh axis runs over, the one named last changes fastest.
Arguments:
- queries: bfloat16 [8, 16, 2048], P('req', None, 'head'), may hold values from -6 to 6
- forget_logits: bfloat16 [8, 16, 2048], P('req', None, 'head'), may hold values from -8 to 8
- values: bfloat16 [8, 16, 2048], P('req', None, 'head'), may hold values from -6 to 6
- gate_input: bfloat16 [8, 16, 2048], P('req', None, 'head'), may hold values from -6 to 6
- init_states: float32 [8, 16, 128, 128], P('req', 'head'), may hold values from -4 to 4
- norm_gain: float32 [128], replicated, may hold values from 0.1 to 1.9
- out_weight: bfloat16 [2048, 2048], P('head'), may hold values from -0.125 to 0.125
- dealing: int32 [8], P('req'), may hold values from 0 to 7, as said below
- accepted: int32 [8], P('req'), may hold values from 0 to 16, as said below
Outputs:
- verified: bfloat16 [8, 16, 2048], P('req', None, 'head')
- new_states: float32 [8, 16, 128, 128], P('req', 'head')
Inputs may be any that keep to these rules, and one draw needn't show every extreme that they name: `dealing`: each request appears in exactly one dealt slot. `accepted`: some request accepts all 16 draft tokens and some accepts none.
All inputs are finite; a program needn't handle non-finite values.
Results may differ from a plain program's by a relative error of at most 0.0049.
Values may be sent and summed in bfloat16 or wider, within the bound.
A program may use at most 64 MiB of HBM per device.

v0:
```python
import jax
import jax.numpy as jnp
from jax import lax
from jax.sharding import PartitionSpec as P

lower_bound = 0.8
norm_eps = 1e-05


def route_gathered(token_tuple, deal_all, worker, local_count):
    mine = worker * local_count + jnp.arange(local_count, dtype=jnp.int32)
    shard_rows = (
        lax.all_gather(token_tuple[0], "req", axis=0, tiled=True),
        lax.all_gather(token_tuple[1], "req", axis=0, tiled=True),
        lax.all_gather(token_tuple[2], "req", axis=0, tiled=True),
        lax.all_gather(token_tuple[3], "req", axis=0, tiled=True),
    )
    match = (deal_all[None, :] == mine[:, None]).astype(jnp.bfloat16)
    totals = tuple(
        (
            jnp.einsum("rk,kte->rte", match, rows, preferred_element_type=jnp.float32)
            for rows in shard_rows
        )
    )
    return tuple((acc.astype(jnp.bfloat16) for acc in totals))


def per_device(
    queries,
    forget_logits,
    values,
    gate_input,
    init_states,
    norm_gain,
    out_weight,
    dealing,
    accepted,
):
    local_count = queries.shape[0]
    draft_len = queries.shape[1]
    head_local = init_states.shape[1]
    head_size = init_states.shape[3]
    deal_all = lax.all_gather(dealing, "req", axis=0, tiled=True)
    worker = lax.axis_index("req")
    token_tuple = (queries, forget_logits, values, gate_input)
    tokens_q, tokens_f, tokens_v, tokens_g = route_gathered(
        token_tuple, deal_all, worker, local_count
    )

    def heads_of(tensor):
        return jnp.moveaxis(
            tensor.astype(jnp.float32).reshape(local_count, draft_len, head_local, head_size), 1, 0
        )

    query_seq = heads_of(tokens_q)
    forget_seq = lower_bound + (1.0 - lower_bound) * jax.nn.sigmoid(heads_of(tokens_f))
    value_seq = heads_of(tokens_v)
    numbers = jnp.arange(1, draft_len + 1, dtype=jnp.int32)

    def advance(state_pair, inputs):
        current, chosen = state_pair
        query_now, forget_now, value_now, number = inputs
        current = (
            forget_now[..., None] * current
            + (1.0 - forget_now)[..., None] * value_now[..., None, :]
        )
        chosen = jnp.where((accepted == number)[:, None, None, None], current, chosen)
        output = jnp.einsum("rhk,rhkv->rhv", query_now, current, precision=lax.Precision.HIGHEST)
        return ((current, chosen), output)

    (last_state, new_states), outputs = lax.scan(
        advance, (init_states, init_states), (query_seq, forget_seq, value_seq, numbers)
    )
    outputs = jnp.moveaxis(outputs, 0, 1)
    meansq = jnp.mean(outputs * outputs, axis=-1, keepdims=True)
    gate_heads = tokens_g.astype(jnp.float32).reshape(local_count, draft_len, head_local, head_size)
    mixed_rows = (
        outputs * lax.rsqrt(meansq + norm_eps) * norm_gain * jax.nn.silu(gate_heads)
    ).astype(jnp.bfloat16)
    mixed_rows = mixed_rows.reshape(local_count * draft_len, head_local * head_size)
    partial_out = jnp.dot(mixed_rows, out_weight, preferred_element_type=jnp.float32)
    summed = lax.psum_scatter(partial_out, "head", scatter_dimension=1, tiled=True)
    verified = summed.astype(jnp.bfloat16).reshape(local_count, draft_len, summed.shape[1])
    return (verified, new_states)


def solution(mesh):
    placed = (
        P("req", None, "head"),
        P("req", None, "head"),
        P("req", None, "head"),
        P("req", None, "head"),
        P("req", "head", None, None),
        P(),
        P("head", None),
        P("req"),
        P("req"),
    )
    return jax.shard_map(
        per_device,
        mesh=mesh,
        in_specs=placed,
        out_specs=(P("req", None, "head"), P("req", "head", None, None)),
        check_vma=False,
    )
```

profile of v0, /device:TPU:0, one launch (start us, length us, event | category | flops | bytes accessed | tf_op | source)
XLA Modules:
  0.0 216.0 jit_solution(8725543321808566249)
XLA Ops:
  7.2 1.1 copy.69
  9.0 1.2 dynamic-slice
  10.2 0.8 dynamic-update-slice
  11.0 13.1 %all-reduce = s32[8]{0:T(128)S(1)} all-reduce(s32[8]{0:T(128)S(1)} %dynamic-update-slice), channel_id=1, replica_groups=mesh['req'=8,'head'=4] {'req'}, use_global_device_ids=true, to_apply=%add | all-reduce | flops 8 | bytes 64
  24.0 30.7 %all_gather.17 = bf16[8,16,512]{2,1,0:T(8,128)(2,1)S(1)} all-gather(bf16[1,16,512]{2,1,0:T(8,128)(2,1)} %param.13), channel_id=1, replica_groups=mesh['req'=8,'head'=4] {'req'}, dimensions={0}, use_global_device_ids=true | all-gather | bytes 147456 | tf_op jit(solution)/shard_map/all_gather | solution.py:15
  55.0 30.7 %all_gather.18 = bf16[8,16,512]{2,1,0:T(8,128)(2,1)S(1)} all-gather(bf16[1,16,512]{2,1,0:T(8,128)(2,1)} %param.11), channel_id=1, replica_groups=mesh['req'=8,'head'=4] {'req'}, dimensions={0}, use_global_device_ids=true | all-gather | bytes 147456 | tf_op jit(solution)/shard_map/all_gather | solution.py:13
  86.0 30.7 %all_gather.16 = bf16[8,16,512]{2,1,0:T(8,128)(2,1)S(1)} all-gather(bf16[1,16,512]{2,1,0:T(8,128)(2,1)} %param.12), channel_id=1, replica_groups=mesh['req'=8,'head'=4] {'req'}, dimensions={0}, use_global_device_ids=true | all-gather | bytes 147456 | tf_op jit(solution)/shard_map/all_gather | solution.py:14
  117.0 40.8 %while.14 = (s32[]{:T(128)}, f32[1,4,128,128]{3,2,1,0:T(8,128)S(1)}, f32[1,4,128,128]{3,2,1,0:T(8,128)S(1)}, f32[16,1,4,128]{3,2,1,0:T(4,128)S(1)}, f32[16,1,4,1...) while((s32[]{:T(128)}, ...), condition=%wide.region_1.2_spmd, body=%wide.region_0.1_spmd.sunk | while | flops 1049091 | bytes 1339531 | solution.py:71
  117.0 0.6 dynamic_slice.23
  118.9 0.3 broadcast_select_fusion.2
  119.2 0.3 fusion.34
  119.6 0.6 dynamic_slice.23
  121.5 0.3 broadcast_select_fusion.2
  121.8 0.3 fusion.34
  122.1 0.6 dynamic_slice.23
  124.0 0.3 broadcast_select_fusion.2
  124.3 0.3 fusion.34
  124.7 0.6 dynamic_slice.23
  126.6 0.3 broadcast_select_fusion.2
  126.9 0.3 fusion.34
  127.2 0.6 dynamic_slice.23
  129.4 0.3 fusion.34
  129.8 0.6 dynamic_slice.23
  132.0 0.3 fusion.34
  132.3 0.6 dynamic_slice.23
  134.5 0.3 fusion.34
  134.8 0.6 dynamic_slice.23
  137.1 0.3 fusion.34
  137.4 0.6 dynamic_slice.23
  139.6 0.3 fusion.34
  139.9 0.6 dynamic_slice.23
  142.2 0.3 fusion.34
  142.5 0.6 dynamic_slice.23
  144.7 0.3 fusion.34
  145.0 0.6 dynamic_slice.23
  147.3 0.3 fusion.34
  147.6 0.6 dynamic_slice.23
  149.8 0.3 fusion.34
  150.1 0.6 dynamic_slice.23
  152.3 0.3 fusion.34
  152.7 0.6 dynamic_slice.23
  154.9 0.3 fusion.34
  155.2 0.6 dynamic_slice.23
  157.4 0.3 fusion.34
  157.9 30.5 %all_gather.19 = bf16[8,16,512]{2,1,0:T(8,128)(2,1)S(1)} all-gather(bf16[1,16,512]{2,1,0:T(8,128)(2,1)S(1)} %copy-done.2), channel_id=1, replica_groups=mesh['req'=8,'head'=4] {'req'}, dimensions={0}, use_global_device_ids=true | all-gather | bytes 147456 | tf_op jit(solution)/shard_map/all_gather | solution.py:16
  188.7 1.0 fusion.16
  189.8 18.0 %reduce-scatter.2.cloned.1.call-done = f32[16,512]{1,0:T(8,128)} async-done(((f32[16,2048]{1,0:T(8,128)}), f32[16,512]{1,0:T(8,128)}) %reduce-scatter.2.cloned.1.call-update) | async-done | bytes 32784 | tf_op jit(solution)/shard_map/reduce_scatter | solution.py:82
  207.8 1.4 convert_bitcast_fusion
  (104 shorter events, 5.0 us)
Async XLA Ops:
  7.2 181.6 %copy-start = (bf16[512,2048]{1,0:T(8,128)(2,1)S(1)}, bf16[512,2048]{1,0:T(8,128)(2,1)}, u32[]{:S(2)}) copy-start(bf16[512,2048]{1,0:T(8,128)(2,1)} %param.17) | copy-start | bytes 6291460
  7.2 200.6 %reduce-scatter.2.cloned.1.call-start = ((), (), s32[]{:S(2)}) async-start(), calls=%async_computation.1 | async-start | bytes 163840 | tf_op jit(solution)/shard_map/reduce_scatter | solution.py:82
  117.0 40.9 %copy-start.2 = (bf16[1,16,512]{2,1,0:T(8,128)(2,1)S(1)}, bf16[1,16,512]{2,1,0:T(8,128)(2,1)}, u32[]{:S(2)}) copy-start(bf16[1,16,512]{2,1,0:T(8,128)(2,1)} %param.14) | copy-start | bytes 49156
  117.0 71.6 %copy-start.3 = (f32[128]{0:T(128)S(1)}, f32[128]{0:T(128)}, u32[]{:S(2)}) copy-start(f32[128]{0:T(128)} %param.16) | copy-start | bytes 1540
  157.8 51.4 %copy-start.1 = (f32[1,4,128,128]{3,2,1,0:T(8,128)}, f32[1,4,128,128]{3,2,1,0:T(8,128)S(1)}, u32[]{:S(2)}) copy-start(f32[1,4,128,128]{3,2,1,0:T(8,128)S(1)} %get-tuple-element.49) | copy-start | bytes 786436
Sparse Core Ops, SparseCore 0:
  189.9 17.8 reduce-scatter.1
where the time goes:
time: 217 us; the launch traced here: 216 us
  blocking collectives  136 us (63%)
  loops' own time  21.3 us (10%)
  waiting for transfers between devices  18 us (8%)
  between operations  14.8 us (7%)
  local copies, waits for them, and re-layouts  13.2 us (6%)
  matrix products  6.86 us (3%)
  other arithmetic  6.03 us (3%)
    all_gather x1, blocking collectives, route_gathered(): lax.all_gather(token_tuple[0], 'req', axis=0, tiled=True)  30.7 us
    all_gather x1, blocking collectives, route_gathered(): lax.all_gather(token_tuple[1], 'req', axis=0, tiled=True)  30.7 us
    all_gather x1, blocking collectives, route_gathered(): lax.all_gather(token_tuple[2], 'req', axis=0, tiled=True)  30.7 us
    all_gather x1, blocking collectives, route_gathered(): lax.all_gather(token_tuple[3], 'req', axis=0, tiled=True)  30.5 us
    another operation x1, loops' own time, per_device(): lax.scan(advance, (init_states, init_states), (query_seq, forget_seq, val...  21.3 us
    reduce_scatter x1, waiting for transfers between devices, per_device(): lax.psum_scatter(partial_out, 'head', scatter_dimension=1, tiled=True)  18 us
    unnamed x1, blocking collectives  13.1 us
    dynamic_slice x32, local copies, waits for them, and re-layouts, per_device(): lax.scan(advance, (init_states, init_states), (query_seq, forget_seq, val...  9.58 us
  transfers between devices with their start and end apart: 1, of which 1 were waited for; matrix products, arithmetic and copies ran while one was open for 0% of the time, Pallas kernels for 0%

commit v1 on v0

v1 whole, which is shorter than its diff:
```python
import functools

import jax
import jax.numpy as jnp
from jax import lax
from jax.experimental import pallas as pl
from jax.experimental.pallas import tpu as pltpu
from jax.sharding import PartitionSpec as P

lower_bound = 0.8
norm_eps = 1e-05
MESH = pl.DeviceIdType.MESH
CHUNKS = 2


def split(x):
    high = x.astype(jnp.bfloat16)
    return high, (x - high.astype(jnp.float32)).astype(jnp.bfloat16)


def mm(a, b, dims=((1,), (0,))):
    return lax.dot_general(a, b, (dims, ((), ())), preferred_element_type=jnp.float32)


def running_product(x):
    rows = lax.broadcasted_iota(jnp.int32, x.shape, 0)
    step = 1
    while step < x.shape[0]:
        x = x * jnp.where(rows >= step, pltpu.roll(x, step, 0), 1.0)
        step *= 2
    return x


def kernel(
    n_req,
    n_head,
    inner,
    q_hbm,
    f_hbm,
    v_hbm,
    g_hbm,
    s_hbm,
    gain_ref,
    w_hbm,
    dealing_ref,
    accepted_ref,
    out_ref,
    new_hbm,
    gath,
    deals,
    cross_out,
    cross_in,
    own,
    states,
    states_high,
    states_low,
    new_states,
    weight,
    keys,
    decay,
    total,
    part_out,
    part_in,
    load_sem,
    state_sem,
    weight_sem,
    store_sem,
    deal_send,
    deal_recv,
    line_send,
    line_recv,
    cross_send,
    cross_recv,
    part_send,
    part_recv,
):
    outer = n_req // inner
    chunks, _, draft, width = gath.shape[1:]
    heads, size = states.shape[0], states.shape[2]
    per = heads // chunks
    columns = out_ref.shape[2]
    me = lax.axis_index("req")
    mine = lax.axis_index("head")
    place = me // inner
    lane = lax.rem(me, inner)
    across = place * inner + (inner - 1 - lane)
    line = [(lax.rem(place + k, outer), lax.rem(place + outer - k, outer)) for k in range(1, outer)]
    ring = [lax.rem(mine + k, n_head) for k in range(1, n_head)]

    loads = []
    for c in range(chunks):
        for a, ref in enumerate((q_hbm, f_hbm, v_hbm, g_hbm)):
            loads.append(
                pltpu.make_async_copy(
                    ref.at[0, :, pl.ds(c * width, width)], gath.at[place, c, a], load_sem.at[c, a]
                )
            )
            loads[-1].start()
    state_copy = pltpu.make_async_copy(s_hbm.at[0], states, state_sem)
    state_copy.start()
    weight_copy = pltpu.make_async_copy(w_hbm, weight, weight_sem)
    weight_copy.start()

    barrier = pltpu.get_barrier_semaphore()
    count = 0
    for to, _ in line:
        pl.semaphore_signal(
            barrier, inc=1, device_id=(to * inner + lane, mine), device_id_type=MESH
        )
        count += 1
    if inner > 1:
        pl.semaphore_signal(barrier, inc=1, device_id=(across, mine), device_id_type=MESH)
        count += 1
    for to in ring:
        pl.semaphore_signal(barrier, inc=1, device_id=(me, to), device_id_type=MESH)
        count += 1
    deals[place] = jnp.full(deals.shape[1:], dealing_ref[0], jnp.int32)
    pl.semaphore_wait(barrier, count)

    def deal_copy(k, slot, to):
        return pltpu.make_async_remote_copy(
            src_ref=deals.at[slot],
            dst_ref=deals.at[slot],
            send_sem=deal_send.at[k],
            recv_sem=deal_recv.at[slot],
            device_id=(to * inner + lane, mine),
            device_id_type=MESH,
        )

    def line_copy(k, c, slot, to):
        return pltpu.make_async_remote_copy(
            src_ref=gath.at[slot, c],
            dst_ref=gath.at[slot, c],
            send_sem=line_send.at[k, c],
            recv_sem=line_recv.at[slot, c],
            device_id=(to * inner + lane, mine),
            device_id_type=MESH,
        )

    for k, (to, _) in enumerate(line):
        deal_copy(k, place, to).start()
    for c in range(chunks):
        for a in range(4):
            loads[c * 4 + a].wait()
        for k, (to, _) in enumerate(line):
            line_copy(k, c, place, to).start()

    state_copy.wait()
    for h in range(heads):
        states_high[h], states_low[h] = split(states[h])

    for k, (to, source) in enumerate(line):
        deal_copy(k, source, to).wait_recv()

    def mask_of(slot, target):
        hit = jnp.where(deals[slot] == target, 1.0, 0.0)
        hit = jnp.concatenate([hit] * (draft // 8), axis=0).astype(jnp.bfloat16)
        return jnp.concatenate([hit] * (width // 128), axis=1)

    masks_own = [mask_of(slot, me) for slot in range(outer)]
    masks_across = [mask_of(slot, across) for slot in range(outer)] if inner > 1 else None

    def pick(masks, c, a):
        acc = masks[0] * gath[0, c, a]
        for slot in range(1, outer):
            acc = acc + masks[slot] * gath[slot, c, a]
        return acc

    def cross_copy(c):
        return pltpu.make_async_remote_copy(
            src_ref=cross_out.at[c],
            dst_ref=cross_in.at[c],
            send_sem=cross_send.at[c],
            recv_sem=cross_recv.at[c],
            device_id=(across, mine),
            device_id_type=MESH,
        )

    def route(c):
        for k, (to, source) in enumerate(line):
            line_copy(k, c, source, to).wait_recv()
        if inner > 1:
            for a in range(4):
                cross_out[c, a] = pick(masks_across, c, a)
            cross_copy(c).start()
        for a in range(4):
            own[c, a] = pick(masks_own, c, a)

    row = lax.broadcasted_iota(jnp.int32, (draft, draft), 0)
    column = lax.broadcasted_iota(jnp.int32, (draft, draft), 1)
    causal = row >= column

    def mix(c):
        if inner > 1:
            cross_copy(c).wait_recv()
            q, f, v, g = (own[c, a] + cross_in[c, a] for a in range(4))
            own[c, 2] = v
        else:
            q, f, v, g = (own[c, a] for a in range(4))
        forget = lower_bound + (1.0 - lower_bound) * jax.nn.sigmoid(f.astype(jnp.float32))
        products = running_product(forget)
        scaled = q.astype(jnp.float32) * products
        key = (1.0 - forget) / products
        decay[c] = products
        keys[c] = key
        gate = g.astype(jnp.float32)
        gate = gate * jax.nn.sigmoid(gate)
        q_high, q_low = split(scaled)
        k_high, k_low = split(key)
        results = []
        for i in range(per):
            h = c * per + i
            s = slice(i * size, (i + 1) * size)
            qh, ql = q_high[:, s], q_low[:, s]
            kh, kl = k_high[:, s], k_low[:, s]
            both = jnp.concatenate([qh, ql], axis=0)
            nt = ((1,), (1,))
            scores = mm(both, kh, nt)
            scores = scores[:draft] + scores[draft:] + mm(qh, kl, nt)
            scores = jnp.where(causal, scores, 0.0)
            a_high, a_low = split(scores)
            carried = mm(both, states_high[h])
            carried = carried[:draft] + carried[draft:] + mm(qh, states_low[h])
            local = mm(jnp.concatenate([a_high, a_low], axis=0), v[:, s])
            o = carried + local[:draft] + local[draft:]
            meansq = jnp.mean(o * o, axis=-1, keepdims=True)
            results.append(o * lax.rsqrt(meansq + norm_eps) * gain_ref[...] * gate[:, s])
        mixed = jnp.concatenate(results, axis=1).astype(jnp.bfloat16)
        return mixed

    def project(c, mixed, last):
        rows = pl.ds(c * width, width)
        for j in range(n_head):
            part = mm(mixed, weight[rows, j * columns : (j + 1) * columns])
            if c > 0:
                part = part + total[j]
            total[j] = part
            if last:
                part_out[j] = part.astype(jnp.bfloat16)

    def store_copy(h):
        return pltpu.make_async_copy(new_states.at[h], new_hbm.at[0, h], store_sem.at[h])

    def advance(c):
        taken = accepted_ref[0]
        rows = lax.broadcasted_iota(jnp.int32, (draft, width), 0)
        last = jnp.sum(jnp.where(rows == taken - 1, decay[c], 0.0), axis=0, keepdims=True)
        last = jnp.where(taken == 0, 1.0, last)
        key = jnp.where(rows < taken, keys[c] * last, 0.0)
        k_high, k_low = split(key)
        both = jnp.concatenate([k_high, k_low], axis=0)
        v = own[c, 2]
        twice = jnp.concatenate([v, v], axis=0)
        for i in range(per):
            h = c * per + i
            s = slice(i * size, (i + 1) * size)
            fade = jnp.broadcast_to(last[:, s], (size, size)).T
            new_states[h] = fade * states[h] + mm(both[:, s], twice[:, s], ((0,), (0,)))
            store_copy(h).start()

    def part_copy(k, slot, to):
        return pltpu.make_async_remote_copy(
            src_ref=part_out.at[to],
            dst_ref=part_in.at[slot],
            send_sem=part_send.at[k],
            recv_sem=part_recv.at[slot],
            device_id=(me, to),
            device_id_type=MESH,
        )

    for c in range(chunks):
        route(c)
        if c > 0:
            advance(c - 1)
        mixed = mix(c)
        if c == 0:
            weight_copy.wait()
        project(c, mixed, c == chunks - 1)
    for k, to in enumerate(ring):
        part_copy(k, mine, to).start()
    advance(chunks - 1)
    result = total[mine]
    for k in range(n_head - 1):
        source = lax.rem(mine + n_head - 1 - k, n_head)
        part_copy(k, source, ring[k]).wait_recv()
        result = result + part_in[source].astype(jnp.float32)
    out_ref[0] = result.astype(jnp.bfloat16)

    for k, (to, _) in enumerate(line):
        deal_copy(k, place, to).wait_send()
        for c in range(chunks):
            line_copy(k, c, place, to).wait_send()
    if inner > 1:
        for c in range(chunks):
            cross_copy(c).wait_send()
    for k, to in enumerate(ring):
        part_copy(k, mine, to).wait_send()
    for h in range(heads):
        store_copy(h).wait()


def per_device(n_req, n_head, *args):
    queries, forget_logits, values, gate_input, states, gain, weight, dealing, accepted = args
    draft, features = queries.shape[1:]
    heads, size = states.shape[1:3]
    columns = weight.shape[1] // n_head
    inner = 2 if n_req % 2 == 0 else 1
    outer = n_req // inner
    chunks = CHUNKS if heads % CHUNKS == 0 else 1
    width = features // chunks
    bf16, f32 = jnp.bfloat16, jnp.float32
    anywhere = pl.BlockSpec(memory_space=pl.ANY)
    vmem = pl.BlockSpec(memory_space=pltpu.VMEM)
    smem = pl.BlockSpec(memory_space=pltpu.SMEM)
    dma = pltpu.SemaphoreType.DMA
    return pl.pallas_call(
        functools.partial(kernel, n_req, n_head, inner),
        out_shape=(
            jax.ShapeDtypeStruct((1, draft, columns), bf16),
            jax.ShapeDtypeStruct(states.shape, f32),
        ),
        in_specs=[anywhere] * 5 + [vmem, anywhere, smem, smem],
        out_specs=(vmem, anywhere),
        scratch_shapes=[
            pltpu.VMEM((outer, chunks, 4, draft, width), bf16),
            pltpu.VMEM((outer, 8, 128), jnp.int32),
            pltpu.VMEM((chunks, 4, draft, width), bf16),
            pltpu.VMEM((chunks, 4, draft, width), bf16),
            pltpu.VMEM((chunks, 4, draft, width), bf16),
            pltpu.VMEM((heads, size, size), f32),
            pltpu.VMEM((heads, size, size), bf16),
            pltpu.VMEM((heads, size, size), bf16),
            pltpu.VMEM((heads, size, size), f32),
            pltpu.VMEM(weight.shape, bf16),
            pltpu.VMEM((chunks, draft, width), f32),
            pltpu.VMEM((chunks, draft, width), f32),
            pltpu.VMEM((n_head, draft, columns), f32),
            pltpu.VMEM((n_head, draft, columns), bf16),
            pltpu.VMEM((n_head, draft, columns), bf16),
            dma((chunks, 4)),
            dma,
            dma,
            dma((heads,)),
            dma((outer,)),
            dma((outer,)),
            dma((outer, chunks)),
            dma((outer, chunks)),
            dma((chunks,)),
            dma((chunks,)),
            dma((n_head,)),
            dma((n_head,)),
        ],
        compiler_params=pltpu.CompilerParams(
            collective_id=0, has_side_effects=True, vmem_limit_bytes=48 * 1024 * 1024
        ),
    )(
        queries,
        forget_logits,
        values,
        gate_input,
        states,
        gain.reshape(1, -1),
        weight,
        dealing,
        accepted,
    )


def solution(mesh):
    placed = (
        P("req", None, "head"),
        P("req", None, "head"),
        P("req", None, "head"),
        P("req", None, "head"),
        P("req", "head", None, None),
        P(),
        P("head", None),
        P("req"),
        P("req"),
    )
    return jax.shard_map(
        functools.partial(per_device, mesh.shape["req"], mesh.shape["head"]),
        mesh=mesh,
        in_specs=placed,
        out_specs=(P("req", None, "head"), P("req", "head", None, None)),
        check_vma=False,
    )
```

time: 217 us -> 31.4 us (0.14)
  blocking collectives: 136 us -> 0 us
  Pallas kernels: 0 us -> 21.6 us
  loops' own time: 21.3 us -> 0 us
  waiting for transfers between devices: 18 us -> 0 us
  between operations: 14.8 us -> 1.95 us
  matrix products: 6.86 us -> 0 us
  other arithmetic: 6.03 us -> 0 us
  local copies, waits for them, and re-layouts: 13.2 us -> 7.37 us
    all_gather x4 -> x0, blocking collectives: 123 us -> none  [the longest x1 30.7 us: route_gathered(): lax.all_gather(token_tuple[0], 'req', axis=0, tiled=True)]
    pallas_call x0 -> x1, Pallas kernels: none -> 21.6 us  [per_device(): pl.pallas_call(functools.partial(kernel, n_req, n_head, inner), out_shape...]
    another operation x1 -> x0, loops' own time: 21.3 us -> none  [per_device(): lax.scan(advance, (init_states, init_states), (query_seq, forget_seq, val...]
    reduce_scatter x1 -> x0, waiting for transfers between devices: 18 us -> none  [per_device(): lax.psum_scatter(partial_out, 'head', scatter_dimension=1, tiled=True)]
    unnamed x1 -> x0, blocking collectives: 13.1 us -> none
    dynamic_slice x32 -> x0, local copies, waits for them, and re-layouts: 9.58 us -> none  [per_device(): lax.scan(advance, (init_states, init_states), (query_seq, forget_seq, val...]
    dot_general x21 -> x0, matrix products: 6.86 us -> none  [the longest x16 5.06 us: advance(): jnp.einsum('rhk,rhkv->rhv', query_now, current, precision=lax.Precision.H...]
    select_n x16 -> x0, other arithmetic: 4.48 us -> none  [advance(): jnp.where((accepted == number)[:, None, None, None], current, chosen)]
  transfers between devices with their start and end apart: 1 -> 0, of which waited for: 1 -> 0; matrix products, arithmetic and copies ran while one was open for 0% -> 0% of each run, Pallas kernels for 0% -> 0%
where the time goes in v1:
time: 31.4 us; the launch traced here: 30.9 us
  Pallas kernels  21.6 us (69%)
  local copies, waits for them, and re-layouts  7.37 us (23%)
  between operations  1.95 us (6%)
    pallas_call x1, Pallas kernels, per_device(): pl.pallas_call(functools.partial(kernel, n_req, n_head, inner), out_shape...  21.6 us
    unnamed x16, local copies, waits for them, and re-layouts  7.37 us

profile of v1, /device:TPU:0, one launch (start us, length us, event | category | flops | bytes accessed | tf_op | source)
XLA Modules:
  0.0 30.9 jit_solution(2006828362357886133)
XLA Ops:
  1.9 0.0 copy-start
  1.9 1.6 %copy-done = bf16[512,2048]{1,0:T(8,128)(2,1)S(1)} copy-done((bf16[512,2048]{1,0:T(8,128)(2,1)S(1)}, bf16[512,2048]{1,0:T(8,128)(2,1)}, u32[]{:S(2)}) %copy-start) | copy-done | bytes 2097176
  3.5 0.0 copy-start.1
  3.5 0.9 %copy-done.1 = f32[1,4,128,128]{3,2,1,0:T(8,128)S(1)} copy-done((f32[1,4,128,128]{3,2,1,0:T(8,128)S(1)}, f32[1,4,128,128]{3,2,1,0:T(8,128)}, u32[]{:S(2)}) %copy-start.1) | copy-done | bytes 262168
  4.5 0.0 copy-start.2
  4.5 0.7 %copy-done.2 = bf16[1,16,512]{2,1,0:T(8,128)(2,1)S(1)} copy-done((bf16[1,16,512]{2,1,0:T(8,128)(2,1)S(1)}, bf16[1,16,512]{2,1,0:T(8,128)(2,1)}, u32[]{:S(2)}) %copy-start.2) | copy-done | bytes 16408
  5.2 0.0 copy-start.3
  5.2 0.7 %copy-done.3 = bf16[1,16,512]{2,1,0:T(8,128)(2,1)S(1)} copy-done((bf16[1,16,512]{2,1,0:T(8,128)(2,1)S(1)}, bf16[1,16,512]{2,1,0:T(8,128)(2,1)}, u32[]{:S(2)}) %copy-start.3) | copy-done | bytes 16408
  5.9 0.0 copy-start.4
  5.9 0.7 %copy-done.4 = bf16[1,16,512]{2,1,0:T(8,128)(2,1)S(1)} copy-done((bf16[1,16,512]{2,1,0:T(8,128)(2,1)S(1)}, bf16[1,16,512]{2,1,0:T(8,128)(2,1)}, u32[]{:S(2)}) %copy-start.4) | copy-done | bytes 16408
  6.6 0.0 copy-start.5
  6.6 0.7 %copy-done.5 = bf16[1,16,512]{2,1,0:T(8,128)(2,1)S(1)} copy-done((bf16[1,16,512]{2,1,0:T(8,128)(2,1)S(1)}, bf16[1,16,512]{2,1,0:T(8,128)(2,1)}, u32[]{:S(2)}) %copy-start.5) | copy-done | bytes 16408
  7.3 0.0 copy-start.6
  7.3 0.7 %copy-done.6 = f32[128]{0:T(128)S(1)} copy-done((f32[128]{0:T(128)S(1)}, f32[128]{0:T(128)}, u32[]{:S(2)}) %copy-start.6) | copy-done | bytes 536
  8.0 21.6 %shard_map.104 = (bf16[1,16,512]{2,1,0:T(8,128)(2,1)S(1)}, f32[1,4,128,128]{3,2,1,0:T(8,128)S(1)}) custom-call(bf16[1,16,512]{2,1,0:T(8,128)(2,1)S(1)} %copy-done.2, bf16[1,16,512]{2,1,0:T(8,128)(2,1)S(1)} %copy-done.3, bf16[1,16,512]{2,1,0:T(8,128)(2,1)S(1)} %copy-done.4, bf16[1,16,512]{2,1,0:T(8,128)(2,1)S(1)} %copy-done.5, ...), custom_call_target="tpu_custom_call" | custom-call | tf_op jit(solution)/shard_map/pallas_call | solution.py:316
  29.6 0.6 %copy.15 = bf16[1,16,512]{2,1,0:T(8,128)(2,1)} copy(bf16[1,16,512]{2,1,0:T(8,128)(2,1)S(1)} %get-tuple-element.4) | data formatting | bytes 32768
  30.2 0.7 %copy.16 = f32[1,4,128,128]{3,2,1,0:T(8,128)} copy(f32[1,4,128,128]{3,2,1,0:T(8,128)S(1)} %get-tuple-element.5) | data formatting | bytes 524288
Async XLA Ops:
  1.9 1.6 %copy-start = (bf16[512,2048]{1,0:T(8,128)(2,1)S(1)}, bf16[512,2048]{1,0:T(8,128)(2,1)}, u32[]{:S(2)}) copy-start(bf16[512,2048]{1,0:T(8,128)(2,1)} %w_hbm.1) | copy-start | bytes 6291460
  3.5 0.9 %copy-start.1 = (f32[1,4,128,128]{3,2,1,0:T(8,128)S(1)}, f32[1,4,128,128]{3,2,1,0:T(8,128)}, u32[]{:S(2)}) copy-start(f32[1,4,128,128]{3,2,1,0:T(8,128)} %s_hbm.1) | copy-start | bytes 786436
  4.5 0.7 %copy-start.2 = (bf16[1,16,512]{2,1,0:T(8,128)(2,1)S(1)}, bf16[1,16,512]{2,1,0:T(8,128)(2,1)}, u32[]{:S(2)}) copy-start(bf16[1,16,512]{2,1,0:T(8,128)(2,1)} %q_hbm.1) | copy-start | bytes 49156
  5.2 0.7 %copy-start.3 = (bf16[1,16,512]{2,1,0:T(8,128)(2,1)S(1)}, bf16[1,16,512]{2,1,0:T(8,128)(2,1)}, u32[]{:S(2)}) copy-start(bf16[1,16,512]{2,1,0:T(8,128)(2,1)} %f_hbm.1) | copy-start | bytes 49156
  5.9 0.7 %copy-start.4 = (bf16[1,16,512]{2,1,0:T(8,128)(2,1)S(1)}, bf16[1,16,512]{2,1,0:T(8,128)(2,1)}, u32[]{:S(2)}) copy-start(bf16[1,16,512]{2,1,0:T(8,128)(2,1)} %v_hbm.1) | copy-start | bytes 49156
  6.6 0.7 %copy-start.5 = (bf16[1,16,512]{2,1,0:T(8,128)(2,1)S(1)}, bf16[1,16,512]{2,1,0:T(8,128)(2,1)}, u32[]{:S(2)}) copy-start(bf16[1,16,512]{2,1,0:T(8,128)(2,1)} %g_hbm.1) | copy-start | bytes 49156
  7.3 0.7 %copy-start.6 = (f32[128]{0:T(128)S(1)}, f32[128]{0:T(128)}, u32[]{:S(2)}) copy-start(f32[128]{0:T(128)} %param.14) | copy-start | bytes 1540

commit v2 on v1

v2 whole, which is shorter than its diff:
```python
import functools

import jax
import jax.numpy as jnp
from jax import lax
from jax.experimental import pallas as pl
from jax.experimental.pallas import tpu as pltpu
from jax.sharding import PartitionSpec as P

lower_bound = 0.8
norm_eps = 1e-05
MESH = pl.DeviceIdType.MESH
CHUNKS = 4


def split(x):
    high = x.astype(jnp.bfloat16)
    return high, (x - high.astype(jnp.float32)).astype(jnp.bfloat16)


def mm(a, b, dims=((1,), (0,))):
    return lax.dot_general(a, b, (dims, ((), ())), preferred_element_type=jnp.float32)


def running_product(x):
    rows = lax.broadcasted_iota(jnp.int32, x.shape, 0)
    step = 1
    while step < x.shape[0]:
        x = x * jnp.where(rows >= step, pltpu.roll(x, step, 0), 1.0)
        step *= 2
    return x


def kernel(
    n_req,
    n_head,
    inner,
    direct,
    order,
    q_hbm,
    f_hbm,
    v_hbm,
    g_hbm,
    s_hbm,
    gain_hbm,
    w_hbm,
    dealing,
    accepted,
    out_ref,
    new_ref,
    raw,
    gath,
    chosen,
    deals,
    cross_out,
    cross_in,
    own,
    states,
    states_high,
    states_low,
    weight,
    gain,
    keys,
    decay,
    total,
    part_out,
    part_in,
    load_sem,
    small_sem,
    deal_send,
    deal_recv,
    line_send,
    line_recv,
    cross_send,
    cross_recv,
    part_send,
    part_recv,
):
    outer = n_req // inner
    chunks, _, draft, width = raw.shape
    heads, size = states.shape[0], states.shape[2]
    per = heads // chunks
    columns = out_ref.shape[2]
    me = lax.axis_index("req")
    mine = lax.axis_index("head")
    place = me // inner
    lane = lax.rem(me, inner)
    across = place * inner + (inner - 1 - lane)
    line = [(lax.rem(place + k, outer), lax.rem(place + outer - k, outer)) for k in range(1, outer)]
    ring = [lax.rem(mine + k, n_head) for k in range(1, n_head)]

    def start(source, target, sem):
        copy = pltpu.make_async_copy(source, target, sem)
        copy.start()
        return copy

    loads = [None] * chunks
    for c in order:
        loads[c] = [
            start(ref.at[0, :, pl.ds(c * width, width)], raw.at[c, a], load_sem.at[c, a])
            for a, ref in enumerate((q_hbm, f_hbm, v_hbm, g_hbm))
        ]
    barrier = pltpu.get_barrier_semaphore()
    peers = [(to * inner + lane, mine) for to, _ in line]
    if inner > 1:
        peers.append((across, mine))
    peers += [(me, to) for to in ring]
    for peer in peers:
        pl.semaphore_signal(barrier, inc=1, device_id=peer, device_id_type=MESH)
    state_load = start(s_hbm.at[0], states, small_sem.at[0])
    weight_load = start(w_hbm, weight, small_sem.at[1])
    gain_load = start(gain_hbm, gain, small_sem.at[2])
    deals[place] = jnp.full(deals.shape[1:], dealing[0], jnp.int32)
    for c in order:
        for load in loads[c]:
            load.wait()
    pl.semaphore_wait(barrier, len(peers))

    def deal_copy(k, slot, to):
        return pltpu.make_async_remote_copy(
            src_ref=deals.at[place],
            dst_ref=deals.at[slot],
            send_sem=deal_send.at[k],
            recv_sem=deal_recv.at[slot],
            device_id=(to, mine),
            device_id_type=MESH,
        )

    def line_copy(k, c, slot, to):
        return pltpu.make_async_remote_copy(
            src_ref=raw.at[c] if c in direct else chosen.at[to, c],
            dst_ref=gath.at[slot, c],
            send_sem=line_send.at[k, c],
            recv_sem=line_recv.at[slot, c],
            device_id=(to * inner + lane, mine),
            device_id_type=MESH,
        )

    def cross_copy(c):
        return pltpu.make_async_remote_copy(
            src_ref=cross_out.at[c] if c in direct else raw.at[c],
            dst_ref=cross_in.at[c],
            send_sem=cross_send.at[c],
            recv_sem=cross_recv.at[c],
            device_id=(across, mine),
            device_id_type=MESH,
        )

    turned = [c for c in order if c not in direct]
    if inner > 1:
        deal_copy(outer - 1, outer, across).start()
    for k, (to, _) in enumerate(line):
        deal_copy(k, place, to * inner + lane).start()
    for c in turned:
        cross_copy(c).start()
    for c in direct:
        for k, (to, _) in enumerate(line):
            line_copy(k, c, place, to).start()

    def mask_of(slot, target):
        hit = jnp.where(deals[slot] == target, 1.0, 0.0)
        hit = jnp.concatenate([hit] * (draft // 8), axis=0).astype(jnp.bfloat16)
        return jnp.concatenate([hit] * (width // 128), axis=1)

    if turned:
        deal_copy(outer - 1, outer, across).wait_recv()
        first = [mask_of(place, slot * inner + lane) for slot in range(outer)]
        second = [mask_of(outer, slot * inner + lane) for slot in range(outer)]
        for c in turned:
            cross_copy(c).wait_recv()
            for slot in range(outer):
                for a in range(4):
                    chosen[slot, c, a] = first[slot] * raw[c, a] + second[slot] * cross_in[c, a]
            for k, (to, _) in enumerate(line):
                line_copy(k, c, place, to).start()

    state_load.wait()
    for h in range(heads):
        states_high[h], states_low[h] = split(states[h])

    for k, (to, source) in enumerate(line):
        deal_copy(k, source, to * inner + lane).wait_recv()

    def pick(target, c):
        masks = [mask_of(lax.rem(place + k, outer), target) for k in range(outer)]
        for a in range(4):
            acc = masks[0] * raw[c, a]
            for k in range(1, outer):
                acc = acc + masks[k] * gath[lax.rem(place + k, outer), c, a]
            yield a, acc

    def collect(c):
        for k, (to, source) in enumerate(line):
            line_copy(k, c, source, to).wait_recv()

    for c in direct:
        collect(c)
        if inner > 1:
            for a, tokens in pick(across, c):
                cross_out[c, a] = tokens
            cross_copy(c).start()
        for a, tokens in pick(me, c):
            own[c, a] = tokens

    def tokens_of(c):
        if c in direct:
            if inner == 1:
                return [own[c, a] for a in range(4)]
            cross_copy(c).wait_recv()
            return [own[c, a] + cross_in[c, a] for a in range(4)]
        collect(c)
        found = []
        for a in range(4):
            acc = chosen[place, c, a]
            for k in range(1, outer):
                acc = acc + gath[lax.rem(place + k, outer), c, a]
            found.append(acc)
        return found

    row = lax.broadcasted_iota(jnp.int32, (draft, draft), 0)
    column = lax.broadcasted_iota(jnp.int32, (draft, draft), 1)
    causal = row >= column

    def mix(c):
        q, f, v, g = tokens_of(c)
        own[c, 2] = v
        forget = lower_bound + (1.0 - lower_bound) * jax.nn.sigmoid(f.astype(jnp.float32))
        products = running_product(forget)
        scaled = q.astype(jnp.float32) * products
        key = (1.0 - forget) / products
        decay[c] = products
        keys[c] = key
        gate = g.astype(jnp.float32)
        gate = gate * jax.nn.sigmoid(gate)
        q_high, q_low = split(scaled)
        k_high, k_low = split(key)
        results = []
        for i in range(per):
            h = c * per + i
            s = slice(i * size, (i + 1) * size)
            qh, ql = q_high[:, s], q_low[:, s]
            kh, kl = k_high[:, s], k_low[:, s]
            both = jnp.concatenate([qh, ql], axis=0)
            nt = ((1,), (1,))
            scores = mm(both, kh, nt)
            scores = scores[:draft] + scores[draft:] + mm(qh, kl, nt)
            scores = jnp.where(causal, scores, 0.0)
            a_high, a_low = split(scores)
            carried = mm(both, states_high[h])
            carried = carried[:draft] + carried[draft:] + mm(qh, states_low[h])
            local = mm(jnp.concatenate([a_high, a_low], axis=0), v[:, s])
            o = carried + local[:draft] + local[draft:]
            meansq = jnp.mean(o * o, axis=-1, keepdims=True)
            results.append(o * lax.rsqrt(meansq + norm_eps) * gain[...] * gate[:, s])
        return jnp.concatenate(results, axis=1).astype(jnp.bfloat16)

    def project(c, mixed):
        rows = pl.ds(c * width, width)
        for j in range(n_head):
            part = mm(mixed, weight[rows, j * columns : (j + 1) * columns])
            if c != order[0]:
                part = part + total[j]
            total[j] = part
            if c == order[-1]:
                part_out[j] = part.astype(jnp.bfloat16)

    def advance(c):
        taken = accepted[0]
        rows = lax.broadcasted_iota(jnp.int32, (draft, width), 0)
        last = jnp.sum(jnp.where(rows == taken - 1, decay[c], 0.0), axis=0, keepdims=True)
        last = jnp.where(taken == 0, 1.0, last)
        key = jnp.where(rows < taken, keys[c] * last, 0.0)
        k_high, k_low = split(key)
        both = jnp.concatenate([k_high, k_low], axis=0)
        v = own[c, 2]
        twice = jnp.concatenate([v, v], axis=0)
        for i in range(per):
            h = c * per + i
            s = slice(i * size, (i + 1) * size)
            fade = jnp.broadcast_to(last[:, s], (size, size)).T
            new_ref[0, h] = fade * states[h] + mm(both[:, s], twice[:, s], ((0,), (0,)))

    def part_copy(k, slot, to):
        return pltpu.make_async_remote_copy(
            src_ref=part_out.at[to],
            dst_ref=part_in.at[slot],
            send_sem=part_send.at[k],
            recv_sem=part_recv.at[slot],
            device_id=(me, to),
            device_id_type=MESH,
        )

    gain_load.wait()
    weight_load.wait()
    for c in order:
        project(c, mix(c))
    for k, to in enumerate(ring):
        part_copy(k, mine, to).start()
    for c in order:
        advance(c)
    result = total[mine]
    for k in range(n_head - 1):
        source = lax.rem(mine + n_head - 1 - k, n_head)
        part_copy(k, source, ring[k]).wait_recv()
        result = result + part_in[source].astype(jnp.float32)
    out_ref[0] = result.astype(jnp.bfloat16)

    if inner > 1:
        deal_copy(outer - 1, outer, across).wait_send()
    for k, (to, _) in enumerate(line):
        deal_copy(k, place, to * inner + lane).wait_send()
        for c in range(chunks):
            line_copy(k, c, place, to).wait_send()
    if inner > 1:
        for c in range(chunks):
            cross_copy(c).wait_send()
    for k, to in enumerate(ring):
        part_copy(k, mine, to).wait_send()


def per_device(n_req, n_head, *args):
    queries, forget_logits, values, gate_input, states, gain, weight, dealing, accepted = args
    draft, features = queries.shape[1:]
    heads, size = states.shape[1:3]
    columns = weight.shape[1] // n_head
    inner = 2 if n_req % 2 == 0 else 1
    outer = n_req // inner
    chunks = CHUNKS if heads % CHUNKS == 0 else 1
    direct = (0,) if inner > 1 else tuple(range(chunks))
    order = (1, 0, 2, 3) if chunks == 4 else tuple(range(chunks))
    width = features // chunks
    bf16, f32 = jnp.bfloat16, jnp.float32
    hbm = pl.BlockSpec(memory_space=pltpu.HBM)
    vmem = pl.BlockSpec(memory_space=pltpu.VMEM)
    smem = pl.BlockSpec(memory_space=pltpu.SMEM)
    dma = pltpu.SemaphoreType.DMA
    return pl.pallas_call(
        functools.partial(kernel, n_req, n_head, inner, direct, order),
        out_shape=(
            jax.ShapeDtypeStruct((1, draft, columns), bf16),
            jax.ShapeDtypeStruct(states.shape, f32),
        ),
        in_specs=[hbm] * 7 + [smem] * 2,
        out_specs=(vmem, vmem),
        scratch_shapes=[
            pltpu.VMEM((chunks, 4, draft, width), bf16),
            pltpu.VMEM((outer, chunks, 4, draft, width), bf16),
            pltpu.VMEM((outer, chunks, 4, draft, width), bf16),
            pltpu.VMEM((outer + 1, 8, 128), jnp.int32),
            pltpu.VMEM((chunks, 4, draft, width), bf16),
            pltpu.VMEM((chunks, 4, draft, width), bf16),
            pltpu.VMEM((chunks, 4, draft, width), bf16),
            pltpu.VMEM((heads, size, size), f32),
            pltpu.VMEM((heads, size, size), bf16),
            pltpu.VMEM((heads, size, size), bf16),
            pltpu.VMEM(weight.shape, bf16),
            pltpu.VMEM((1, size), f32),
            pltpu.VMEM((chunks, draft, width), f32),
            pltpu.VMEM((chunks, draft, width), f32),
            pltpu.VMEM((n_head, draft, columns), f32),
            pltpu.VMEM((n_head, draft, columns), bf16),
            pltpu.VMEM((n_head, draft, columns), bf16),
            dma((chunks, 4)),
            dma((3,)),
            dma((outer,)),
            dma((outer + 1,)),
            dma((outer, chunks)),
            dma((outer, chunks)),
            dma((chunks,)),
            dma((chunks,)),
            dma((n_head,)),
            dma((n_head,)),
        ],
        compiler_params=pltpu.CompilerParams(
            collective_id=0, has_side_effects=True, vmem_limit_bytes=56 * 1024 * 1024
        ),
    )(
        queries,
        forget_logits,
        values,
        gate_input,
        states,
        gain.reshape(1, -1),
        weight,
        dealing,
        accepted,
    )


def solution(mesh):
    placed = (
        P("req", None, "head"),
        P("req", None, "head"),
        P("req", None, "head"),
        P("req", None, "head"),
        P("req", "head", None, None),
        P(),
        P("head", None),
        P("req"),
        P("req"),
    )
    return jax.shard_map(
        functools.partial(per_device, mesh.shape["req"], mesh.shape["head"]),
        mesh=mesh,
        in_specs=placed,
        out_specs=(P("req", None, "head"), P("req", "head", None, None)),
        check_vma=False,
    )
```

time: 31.4 us -> 23.1 us (0.74)
  local copies, waits for them, and re-layouts: 7.37 us -> 2.99 us
  Pallas kernels: 21.6 us -> 18 us
    unnamed x16 -> x2, local copies, waits for them, and re-layouts: 7.37 us -> 2.99 us
    pallas_call x1, Pallas kernels: 21.6 us -> 18 us  [per_device(): pl.pallas_call(functools.partial(kernel, n_req, n_head, inner, direct, or...]
where the time goes in v2:
time: 23.1 us; the launch traced here: 22.9 us
  Pallas kernels  18 us (78%)
  local copies, waits for them, and re-layouts  2.99 us (13%)
  between operations  1.93 us (8%)
    pallas_call x1, Pallas kernels, per_device(): pl.pallas_call(functools.partial(kernel, n_req, n_head, inner, direct, or...  18 us
    unnamed x2, local copies, waits for them, and re-layouts  2.99 us

profile of v2, /device:TPU:0, one launch (start us, length us, event | category | flops | bytes accessed | tf_op | source)
XLA Modules:
  0.0 22.9 jit_solution(18218394762976499311)
XLA Ops:
  1.9 18.0 %shard_map.104 = (bf16[1,16,512]{2,1,0:T(8,128)(2,1)}, f32[1,4,128,128]{3,2,1,0:T(8,128)}) custom-call(bf16[1,16,512]{2,1,0:T(8,128)(2,1)} %q_hbm.1, bf16[1,16,512]{2,1,0:T(8,128)(2,1)} %f_hbm.1, bf16[1,16,512]{2,1,0:T(8,128)(2,1)} %v_hbm.1, bf16[1,16,512]{2,1,0:T(8,128)(2,1)} %g_hbm.1, f32[1,4,128,128]{3,2,1,0:T(8,128)} %s_hbm.1, f32[1,128]{1,0:T(1,128)} %bitcast.1, ...), custom_call_target="tpu_custom_call" | custom-call | tf_op jit(solution)/shard_map/pallas_call | solution.py:337
  19.9 1.3 %copy.15 = bf16[1,16,512]{2,1,0:T(8,128)(2,1)} copy(bf16[1,16,512]{2,1,0:T(8,128)(2,1)} %get-tuple-element.4) | data formatting | bytes 32768
  21.2 1.7 %copy.16 = f32[1,4,128,128]{3,2,1,0:T(8,128)} copy(f32[1,4,128,128]{3,2,1,0:T(8,128)} %get-tuple-element.5) | data formatting | bytes 524288

commit v3 on v2

--- a/solution.py
+++ b/solution.py
@@ -372,16 +372,13 @@
             dma((n_head,)),
         ],
         compiler_params=pltpu.CompilerParams(
-            collective_id=0, has_side_effects=True, vmem_limit_bytes=56 * 1024 * 1024
+            collective_id=0, has_side_effects=True, vmem_limit_bytes=24 * 1024 * 1024
         ),
     )(
-        queries,
-        forget_logits,
-        values,
-        gate_input,
-        states,
-        gain.reshape(1, -1),
-        weight,
+        *[
+            pltpu.with_memory_space_constraint(x, pltpu.HBM)
+            for x in (queries, forget_logits, values, gate_input, states, gain.reshape(1, -1), weight)
+        ],
         dealing,
         accepted,
     )

time: 23.1 us -> 20.7 us (0.90)
  local copies, waits for them, and re-layouts: 2.99 us -> 1.31 us
  Pallas kernels: 18 us -> 17.3 us
    unnamed x2, local copies, waits for them, and re-layouts: 2.99 us -> 1.31 us
    pallas_call x1, Pallas kernels: 18 us -> 17.3 us  [per_device(): pl.pallas_call(functools.partial(kernel, n_req, n_head, inner, direct, or...]
where the time goes in v3:
time: 20.7 us; the launch traced here: 20.5 us
  Pallas kernels  17.3 us (84%)
  between operations  1.93 us (9%)
  local copies, waits for them, and re-layouts  1.31 us (6%)
    pallas_call x1, Pallas kernels, per_device(): pl.pallas_call(functools.partial(kernel, n_req, n_head, inner, direct, or...  17.3 us
    unnamed x2, local copies, waits for them, and re-layouts  1.31 us

profile of v3, /device:TPU:0, one launch (start us, length us, event | category | flops | bytes accessed | tf_op | source)
XLA Modules:
  0.0 20.5 jit_solution(3603827371247805404)
XLA Ops:
  1.9 17.3 %shard_map.104 = (bf16[1,16,512]{2,1,0:T(8,128)(2,1)S(1)}, f32[1,4,128,128]{3,2,1,0:T(8,128)S(1)}) custom-call(bf16[1,16,512]{2,1,0:T(8,128)(2,1)} %q_hbm.1, bf16[1,16,512]{2,1,0:T(8,128)(2,1)} %f_hbm.1, bf16[1,16,512]{2,1,0:T(8,128)(2,1)} %v_hbm.1, bf16[1,16,512]{2,1,0:T(8,128)(2,1)} %g_hbm.1, f32[1,4,128,128]{3,2,1,0:T(8,128)} %s_hbm.1, f32[1,128]{1,0:T(1,128)} %bitcast.1, ...), custom_call_target="tpu_custom_call" | custom-call | tf_op jit(solution)/shard_map/pallas_call | solution.py:337
  19.2 0.6 %copy.15 = bf16[1,16,512]{2,1,0:T(8,128)(2,1)} copy(bf16[1,16,512]{2,1,0:T(8,128)(2,1)S(1)} %get-tuple-element.4) | data formatting | bytes 32768
  19.8 0.7 %copy.16 = f32[1,4,128,128]{3,2,1,0:T(8,128)} copy(f32[1,4,128,128]{3,2,1,0:T(8,128)S(1)} %get-tuple-element.5) | data formatting | bytes 524288

commit v4 on v3

--- a/solution.py
+++ b/solution.py
@@ -326,8 +326,8 @@
     inner = 2 if n_req % 2 == 0 else 1
     outer = n_req // inner
     chunks = CHUNKS if heads % CHUNKS == 0 else 1
-    direct = (0,) if inner > 1 else tuple(range(chunks))
-    order = (1, 0, 2, 3) if chunks == 4 else tuple(range(chunks))
+    direct = tuple(range(max(1, chunks // 2))) if inner > 1 else tuple(range(chunks))
+    order = (0, 2, 1, 3) if chunks == 4 else tuple(range(chunks))
     width = features // chunks
     bf16, f32 = jnp.bfloat16, jnp.float32
     hbm = pl.BlockSpec(memory_space=pltpu.HBM)

time: 20.7 us -> 21.9 us (1.058)
  Pallas kernels: 17.3 us -> 18.5 us
    pallas_call x1, Pallas kernels: 17.3 us -> 18.5 us  [per_device(): pl.pallas_call(functools.partial(kernel, n_req, n_head, inner, direct, or...]
where the time goes in v4:
time: 21.9 us; the launch traced here: 21.7 us
  Pallas kernels  18.5 us (84%)
  between operations  1.93 us (9%)
  local copies, waits for them, and re-layouts  1.31 us (6%)
    pallas_call x1, Pallas kernels, per_device(): pl.pallas_call(functools.partial(kernel, n_req, n_head, inner, direct, or...  18.5 us
    unnamed x2, local copies, waits for them, and re-layouts  1.31 us

profile of v4, /device:TPU:0, one launch (start us, length us, event | category | flops | bytes accessed | tf_op | source)
XLA Modules:
  0.0 21.7 jit_solution(4986737428970040609)
XLA Ops:
  1.9 18.5 %shard_map.104 = (bf16[1,16,512]{2,1,0:T(8,128)(2,1)S(1)}, f32[1,4,128,128]{3,2,1,0:T(8,128)S(1)}) custom-call(bf16[1,16,512]{2,1,0:T(8,128)(2,1)} %q_hbm.1, bf16[1,16,512]{2,1,0:T(8,128)(2,1)} %f_hbm.1, bf16[1,16,512]{2,1,0:T(8,128)(2,1)} %v_hbm.1, bf16[1,16,512]{2,1,0:T(8,128)(2,1)} %g_hbm.1, f32[1,4,128,128]{3,2,1,0:T(8,128)} %s_hbm.1, f32[1,128]{1,0:T(1,128)} %bitcast.1, ...), custom_call_target="tpu_custom_call" | custom-call | tf_op jit(solution)/shard_map/pallas_call | solution.py:337
  20.4 0.6 %copy.15 = bf16[1,16,512]{2,1,0:T(8,128)(2,1)} copy(bf16[1,16,512]{2,1,0:T(8,128)(2,1)S(1)} %get-tuple-element.4) | data formatting | bytes 32768
  21.0 0.7 %copy.16 = f32[1,4,128,128]{3,2,1,0:T(8,128)} copy(f32[1,4,128,128]{3,2,1,0:T(8,128)S(1)} %get-tuple-element.5) | data formatting | bytes 524288

commit v5 on v4

--- a/solution.py
+++ b/solution.py
@@ -149,8 +149,9 @@
     turned = [c for c in order if c not in direct]
     if inner > 1:
         deal_copy(outer - 1, outer, across).start()
-    for k, (to, _) in enumerate(line):
-        deal_copy(k, place, to * inner + lane).start()
+    if direct:
+        for k, (to, _) in enumerate(line):
+            deal_copy(k, place, to * inner + lane).start()
     for c in turned:
         cross_copy(c).start()
     for c in direct:
@@ -178,8 +179,9 @@
     for h in range(heads):
         states_high[h], states_low[h] = split(states[h])
 
-    for k, (to, source) in enumerate(line):
-        deal_copy(k, source, to * inner + lane).wait_recv()
+    if direct:
+        for k, (to, source) in enumerate(line):
+            deal_copy(k, source, to * inner + lane).wait_recv()
 
     def pick(target, c):
         masks = [mask_of(lax.rem(place + k, outer), target) for k in range(outer)]
@@ -308,7 +310,8 @@
     if inner > 1:
         deal_copy(outer - 1, outer, across).wait_send()
     for k, (to, _) in enumerate(line):
-        deal_copy(k, place, to * inner + lane).wait_send()
+        if direct:
+            deal_copy(k, place, to * inner + lane).wait_send()
         for c in range(chunks):
             line_copy(k, c, place, to).wait_send()
     if inner > 1:
@@ -326,8 +329,8 @@
     inner = 2 if n_req % 2 == 0 else 1
     outer = n_req // inner
     chunks = CHUNKS if heads % CHUNKS == 0 else 1
-    direct = tuple(range(max(1, chunks // 2))) if inner > 1 else tuple(range(chunks))
-    order = (0, 2, 1, 3) if chunks == 4 else tuple(range(chunks))
+    direct = () if inner > 1 else tuple(range(chunks))
+    order = tuple(range(chunks))
     width = features // chunks
     bf16, f32 = jnp.bfloat16, jnp.float32
     hbm = pl.BlockSpec(memory_space=pltpu.HBM)

time: 21.9 us -> 22 us (level)
  no operation moved by 1% of the time
where the time goes in v5:
time: 22 us; the launch traced here: 21.8 us
  Pallas kernels  18.6 us (85%)
  between operations  1.93 us (9%)
  local copies, waits for them, and re-layouts  1.31 us (6%)
    pallas_call x1, Pallas kernels, per_device(): pl.pallas_call(functools.partial(kernel, n_req, n_head, inner, direct, or...  18.6 us
    unnamed x2, local copies, waits for them, and re-layouts  1.31 us

profile of v5, /device:TPU:0, one launch (start us, length us, event | category | flops | bytes accessed | tf_op | source)
XLA Modules:
  0.0 21.8 jit_solution(14618218907810302139)
XLA Ops:
  1.9 18.6 %shard_map.104 = (bf16[1,16,512]{2,1,0:T(8,128)(2,1)S(1)}, f32[1,4,128,128]{3,2,1,0:T(8,128)S(1)}) custom-call(bf16[1,16,512]{2,1,0:T(8,128)(2,1)} %q_hbm.1, bf16[1,16,512]{2,1,0:T(8,128)(2,1)} %f_hbm.1, bf16[1,16,512]{2,1,0:T(8,128)(2,1)} %v_hbm.1, bf16[1,16,512]{2,1,0:T(8,128)(2,1)} %g_hbm.1, f32[1,4,128,128]{3,2,1,0:T(8,128)} %s_hbm.1, f32[1,128]{1,0:T(1,128)} %bitcast.1, ...), custom_call_target="tpu_custom_call" | custom-call | tf_op jit(solution)/shard_map/pallas_call | solution.py:340
  20.5 0.6 %copy.15 = bf16[1,16,512]{2,1,0:T(8,128)(2,1)} copy(bf16[1,16,512]{2,1,0:T(8,128)(2,1)S(1)} %get-tuple-element.4) | data formatting | bytes 32768
  21.1 0.7 %copy.16 = f32[1,4,128,128]{3,2,1,0:T(8,128)} copy(f32[1,4,128,128]{3,2,1,0:T(8,128)S(1)} %get-tuple-element.5) | data formatting | bytes 524288
